TPU v7x, 256 devices: a whole 4x4x8 slice. The times are simulated.
256 devices in a mesh: row: 8 (over z_hi, x), col: 32 (over z_lo, y, core).
Axes of the slice: x: 4, y: 4, z: 8 (z_hi: 2, z_lo: 4; z = z_hi * 4 + z_lo), core: 2. Of those that a mesh axis runs over, the one named last changes fastest.
Arguments:
- node_features: bfloat16 [32768, 512], P(('row', 'col')), may hold values from -6 to 6
- out_grad: bfloat16 [32768, 512], P(('row', 'col')), may hold values from -6 to 6
- adjacency: bfloat16 [32768, 32768], P('row', 'col'), may hold values from 0 to 1.5, as said below
- tile_mask: int32 [256, 256], P('row', 'col'), may hold values from 0 to 1, as said below
- degrees: int32 [32768], P(('row', 'col')), may hold values from 4 to 15
- w_self: bfloat16 [512, 512], replicated, may hold values from -0.25 to 0.25
- w_neigh: bfloat16 [512, 512], replicated, may hold values from -0.25 to 0.25
Outputs:
- in_grad: bfloat16 [32768, 512], P(('row', 'col'))
- grad_self: float32 [512, 512], replicated
- grad_neigh: float32 [512, 512], replicated
Inputs may be any that keep to these rules, and one draw needn't show every extreme that they name: `adjacency`: zero where there is no edge; about one entry in 32 inside a tile is an edge. `tile_mask`: the share of tiles with edges differs between the blocks of 32 x 8 tiles.
All inputs are finite; a program needn't handle non-finite values.
Results may differ from a plain program's by a relative error of at most 0.0053.
Values may be sent and summed in bfloat16 or wider, within the bound.
A program may use at most 64 MiB of HBM per device.

v0:
```python
import math

import jax
import jax.numpy as jnp
from jax import lax
from jax.sharding import PartitionSpec as P


def local(node_features, out_grad, adjacency, tile_mask, degrees, w_self, w_neigh):
    node_dev, feat_width = node_features.shape
    span_rows, span_cols = adjacency.shape
    tile_rows, tile_cols = tile_mask.shape
    tile_size = span_rows // tile_rows
    blocked = (
        adjacency.reshape(tile_rows, tile_size, tile_cols, tile_size)
        * tile_mask.astype(jnp.bfloat16)[:, None, :, None]
    )
    edge_values = blocked.reshape(span_rows, span_cols)
    scaled = (out_grad.astype(jnp.float32) / degrees.astype(jnp.float32)[:, None]).astype(
        jnp.bfloat16
    )
    spread_total = lax.dot_general(
        edge_values,
        lax.all_gather(scaled, "col", axis=0, tiled=True),
        (((0,), (0,)), ((), ())),
        preferred_element_type=jnp.float32,
    )
    pulled = lax.psum_scatter(spread_total, "row", scatter_dimension=0, tiled=True)
    neigh_part = lax.dot_general(
        node_features.astype(jnp.float32),
        pulled,
        (((0,), (0,)), ((), ())),
        precision=lax.Precision.HIGHEST,
    )
    self_part = lax.dot_general(
        node_features, out_grad, (((0,), (0,)), ((), ())), preferred_element_type=jnp.float32
    )
    self_sum, neigh_sum = lax.psum((self_part, neigh_part), ("row", "col"))
    node_count = node_dev * lax.axis_size("row") * lax.axis_size("col")
    factor = 1.0 / math.sqrt(node_count)
    pulled_half = pulled.astype(jnp.bfloat16)
    own_term = lax.dot_general(
        out_grad, w_self, (((1,), (1,)), ((), ())), preferred_element_type=jnp.float32
    )
    neigh_term = lax.dot_general(
        pulled_half, w_neigh, (((1,), (1,)), ((), ())), preferred_element_type=jnp.float32
    )
    in_grad = (own_term + neigh_term).astype(jnp.bfloat16)
    return (in_grad, self_sum * factor, neigh_sum * factor)


def solution(mesh):
    in_specs = (
        P(("row", "col"), None),
        P(("row", "col"), None),
        P("row", "col"),
        P("row", "col"),
        P(("row", "col")),
        P(),
        P(),
    )
    out_specs = (P(("row", "col"), None), P(), P())
    return jax.shard_map(local, mesh=mesh, in_specs=in_specs, out_specs=out_specs, check_vma=False)
```

profile of v0, /device:TPU:1, one launch (start us, length us, event | category | flops | bytes accessed | tf_op | source)
XLA Modules:
  0.0 455.9 jit_solution(10194192185701506360)
XLA Ops:
  7.2 0.0 copy-start
  7.2 0.0 all-gather.2.cloned.1.call-start
  7.2 0.7 convert_element_type.21
  7.9 1.7 divide_convert_fusion
  9.6 0.0 all-gather.2.cloned.1.call-update
  9.6 0.0 reduce-scatter.2.cloned.1.call-start
  9.7 0.7 convert_element_type.19
  10.4 0.1 copy.10
  10.4 67.1 %all-gather.2.cloned.1.call-done = bf16[4096,512]{1,0:T(8,128)(2,1)} async-done(((bf16[128,512]{1,0:T(8,128)(2,1)}), bf16[4096,512]{1,0:T(8,128)(2,1)}) %all-gather.2.cloned.1.call-update) | async-done | bytes 4194320 | tf_op jit(solution)/shard_map/all_gather | solution.py:24
  77.6 0.0 copy-start.4
  77.6 1.1 mul.17
  78.7 2.2 copy-done.4
  81.0 0.0 copy-start.1
  81.0 0.0 copy-start.3
  81.0 0.0 copy-start.2
  81.0 8.2 %fusion = f32[1024,512]{1,0:T(8,128)} fusion(bf16[4096,512]{1,0:T(8,128)(2,1)} %all-gather.2.cloned.1.call-done, bf16[4096,1024]{1,0:T(8,128)(2,1)S(1)} %copy-done.4, bf16[512,8,8,128]{3,2,1,0:T(8,128)(2,1)S(1)} %bitcast.15), kind=kOutput, calls=%fused_computation.1 | convolution fusion | flops 4299161600 | bytes 23068672 | tf_op jit(solution)/shard_map/dot_general | solution.py:22
  89.2 0.0 reduce-scatter.2.cloned.1.call-update
  89.2 0.0 all-reduce.3.cloned.1.call-start
  89.2 0.0 copy-done.1
  89.3 0.0 copy-done.3
  89.3 1.3 fusion.5
  90.6 91.1 %reduce-scatter.2.cloned.1.call-done = f32[128,512]{1,0:T(8,128)} async-done(((f32[1024,512]{1,0:T(8,128)}), f32[128,512]{1,0:T(8,128)}) %reduce-scatter.2.cloned.1.call-update) | async-done | bytes 262160 | tf_op jit(solution)/shard_map/reduce_scatter | solution.py:28
  181.7 2.5 convolution_bitcast_fusion
  184.2 0.0 all-reduce.3.cloned.1.call-update
  184.2 0.0 copy-done
  184.3 0.3 fusion.4
  184.6 0.0 copy-done.2
  184.6 1.9 fusion.2
  186.5 259.7 %all-reduce.3.cloned.1.call-done = (f32[512,512]{1,0:T(8,128)}, f32[512,512]{1,0:T(8,128)}) async-done(((f32[512,512]{1,0:T(8,128)}, f32[512,512]{1,0:T(8,128)}), (f32[512,512]{1,0:T(8,128)}, f32[512,512]{1,0:T(8,128)})) %all-reduce.3.cloned.1.call-update) | async-done | bytes 2097168 | tf_op jit(solution)/shard_map/psum | solution.py:38
  446.2 3.1 broadcast_multiply_fusion
Async XLA Ops:
  7.2 177.1 %copy-start = (bf16[512,512]{1,0:T(8,128)(2,1)S(1)}, bf16[512,512]{1,0:T(8,128)(2,1)}, u32[]{:S(2)}) copy-start(bf16[512,512]{1,0:T(8,128)(2,1)} %param.12) | copy-start | bytes 1572868
  7.2 70.4 %all-gather.2.cloned.1.call-start = ((), (), s32[]{:S(2)}) async-start(), calls=%async_computation.1 | async-start | bytes 4325376 | tf_op jit(solution)/shard_map/all_gather | solution.py:24
  9.6 172.1 %reduce-scatter.2.cloned.1.call-start = ((), (), s32[]{:S(2)}) async-start(), calls=%async_computation.2 | async-start | bytes 2359296 | tf_op jit(solution)/shard_map/reduce_scatter | solution.py:28
  77.6 3.4 copy-start.4
  81.0 8.3 %copy-start.1 = (bf16[128,512]{1,0:T(8,128)(2,1)S(1)}, bf16[128,512]{1,0:T(8,128)(2,1)}, u32[]{:S(2)}) copy-start(bf16[128,512]{1,0:T(8,128)(2,1)} %param.8) | copy-start | bytes 393220
  81.0 8.3 %copy-start.3 = (bf16[128,512]{1,0:T(8,128)(2,1)S(1)}, bf16[128,512]{1,0:T(8,128)(2,1)}, u32[]{:S(2)}) copy-start(bf16[128,512]{1,0:T(8,128)(2,1)} %param.7) | copy-start | bytes 393220
  81.0 103.6 %copy-start.2 = (bf16[512,512]{1,0:T(8,128)(2,1)S(1)}, bf16[512,512]{1,0:T(8,128)(2,1)}, u32[]{:S(2)}) copy-start(bf16[512,512]{1,0:T(8,128)(2,1)} %param.13) | copy-start | bytes 1572868
  89.2 357.0 %all-reduce.3.cloned.1.call-start = ((), (), s32[]{:S(2)}) async-start(), calls=%async_computation.3 | async-start | bytes 4194304 | tf_op jit(solution)/shard_map/psum | solution.py:38
Sparse Core Ops, SparseCore 0:
  10.4 67.1 all-gather.1
  89.3 92.3 reduce-scatter.1
  188.7 257.4 all-reduce.2
where the time goes:
time: 457 us; the launch traced here: 456 us
  waiting for transfers between devices  418 us (91%)
  matrix products  14.2 us (3%)
  between operations  13.8 us (3%)
  other arithmetic  6.15 us (1%)
    psum x1, waiting for transfers between devices, local(): self_sum, neigh_sum = lax.psum((self_part, neigh_part), ('row', 'col'))  260 us
    reduce_scatter x1, waiting for transfers between devices, local(): lax.psum_scatter(spread_total, 'row', scatter_dimension=0, tiled=True)  91.1 us
    all_gather x1, waiting for transfers between devices, local(): lax.all_gather(scaled, 'col', axis=0, tiled=True)  67.1 us
  transfers between devices with their start and end apart: 3, of which 3 were waited for; matrix products, arithmetic and copies ran while one was open for 1% of the time, Pallas kernels for 0%

commit v1 on v0

v1 whole, which is shorter than its diff:
```python
import math

import jax
import jax.numpy as jnp
from jax import lax
from jax.experimental import pallas as pl
from jax.experimental.pallas import tpu as pltpu
from jax.sharding import PartitionSpec as P

MESH = pl.DeviceIdType.MESH
F32, BF16 = jnp.float32, jnp.bfloat16
FEAT = 512
NODE = 128
PARTS = 2
CHUNK = FEAT // PARTS


def rdma(src, dst, send_sem, recv_sem, to):
    return pltpu.make_async_remote_copy(
        src_ref=src, dst_ref=dst, send_sem=send_sem, recv_sem=recv_sem, device_id=to, device_id_type=MESH
    )


class Place:
    def __init__(self):
        row, col = lax.axis_index("row"), lax.axis_index("col")
        self.row, self.col = row, col
        self.x, self.zh = lax.rem(row, 4), lax.div(row, 4)
        self.zl, self.y, self.k = lax.div(col, 8), lax.rem(lax.div(col, 2), 4), lax.rem(col, 2)
        self.z = self.zh * 4 + self.zl
        self.q = self.x * 4 + self.y

    def at(self, x=None, y=None, z=None, k=None):
        x = self.x if x is None else x
        y = self.y if y is None else y
        z = self.z if z is None else z
        k = self.k if k is None else k
        return (lax.div(z, 4) * 4 + x, lax.rem(z, 4) * 8 + y * 2 + k)

    def chip(self, d):
        q = lax.rem(self.q + d, 16)
        return q, self.at(x=lax.div(q, 4), y=lax.rem(q, 4))

    def along_z(self, d):
        z = lax.rem(self.z + d, 8)
        return z, self.at(z=z)

    def wait_recv(self, ref, sem):
        rdma(ref, ref, sem, sem, self.at()).wait_recv()

    def wait_send(self, ref, sem):
        rdma(ref, ref, sem, sem, self.at()).wait_send()


class Total:
    def __init__(self, place, rows, refs):
        self.place, self.rows, self.lanes, self.across = place, rows, rows, FEAT // rows
        self.part, self.kin, self.out_piece, self.in_piece, self.zbuf, self.whole, self.ss, self.rs = refs

    @staticmethod
    def scratch(rows):
        half = rows // 2
        return [
            pltpu.VMEM((2, half, FEAT), BF16),
            pltpu.VMEM((half, FEAT), BF16),
            pltpu.VMEM((16, 16, rows), BF16),
            pltpu.VMEM((16, 16, rows), BF16),
            pltpu.VMEM((8, 16, rows), BF16),
            pltpu.VMEM((2, 16, 16, rows), BF16),
            pltpu.SemaphoreType.DMA((5,)),
            pltpu.SemaphoreType.DMA((5,)),
        ]

    def spot(self, p):
        return slice((p // self.across) * 16, (p // self.across) * 16 + 16), slice(
            (p % self.across) * self.lanes, (p % self.across + 1) * self.lanes
        )

    def start(self, value):
        pc, half = self.place, self.rows // 2
        self.part[0] = value[:half].astype(BF16)
        self.part[1] = value[half:].astype(BF16)
        rdma(self.part.at[1 - pc.k], self.kin, self.ss.at[0], self.rs.at[0], pc.at(k=1 - pc.k)).start()

    def plane(self):
        pc = self.place
        pc.wait_recv(self.kin, self.rs.at[0])
        both = (self.part[pc.k].astype(F32) + self.kin[...].astype(F32)).astype(BF16)
        for p in range(16):
            self.out_piece[p] = both[self.spot(p)]

        def send(d, _):
            q, to = pc.chip(d)
            rdma(self.out_piece.at[q], self.in_piece.at[pc.q], self.ss.at[1], self.rs.at[1], to).start()
            return _

        lax.fori_loop(1, 16, send, 0)
        self.in_piece[pc.q] = self.out_piece[pc.q]

    def column(self):
        pc = self.place
        pc.wait_recv(self.in_piece.at[pl.ds(0, 15)], self.rs.at[1])
        self.zbuf[pc.z] = jnp.sum(self.in_piece[...].astype(F32), axis=0).astype(BF16)

        def send(d, _):
            z, to = pc.along_z(d)
            rdma(self.zbuf.at[pc.z], self.zbuf.at[pc.z], self.ss.at[2], self.rs.at[2], to).start()
            return _

        lax.fori_loop(1, 8, send, 0)

    def spread(self, factor):
        pc = self.place
        pc.wait_recv(self.zbuf.at[pl.ds(0, 7)], self.rs.at[2])
        self.whole[pc.k, pc.q] = (jnp.sum(self.zbuf[...].astype(F32), axis=0) * factor).astype(BF16)
        mine = self.whole.at[pc.k, pc.q]

        def send(d, _):
            q, to = pc.chip(d)
            rdma(mine, mine, self.ss.at[3], self.rs.at[3], to).start()
            return _

        lax.fori_loop(1, 16, send, 0)

    def cross(self):
        pc = self.place
        pc.wait_recv(self.whole.at[0, pl.ds(0, 15)], self.rs.at[3])
        mine = self.whole.at[pc.k]
        rdma(mine, mine, self.ss.at[4], self.rs.at[4], pc.at(k=1 - pc.k)).start()

    def finish(self, out_ref, base):
        pc, half = self.place, self.rows // 2
        pc.wait_recv(self.whole.at[0], self.rs.at[4])
        for h in range(2):
            for p in range(16):
                rows, lanes = self.spot(p)
                out_ref[base + h * half + rows.start : base + h * half + rows.stop, lanes] = self.whole[h, p]

    def drain(self):
        pc = self.place
        pc.wait_send(self.kin, self.ss.at[0])
        pc.wait_send(self.in_piece.at[pl.ds(0, 15)], self.ss.at[1])
        pc.wait_send(self.zbuf.at[pl.ds(0, 7)], self.ss.at[2])
        pc.wait_send(self.whole.at[0, pl.ds(0, 15)], self.ss.at[3])
        pc.wait_send(self.whole.at[0], self.ss.at[4])


def kernel(factor, *refs):
    nf_ref, og_ref, mask_ref, deg_ref, adj_ref, ws_hbm, wn_hbm = refs[:7]
    ig_ref, gs_ref, gn_ref = refs[7:10]
    (
        adj, wide_mask, gath, lhs, acc, part, rx, zout, zin, own, feats, ws, wn, grad_t, ig_t,
        local_sem, z_ss, z_rs, y_ss, y_rs, k_ss, k_rs, f_ss, f_rs, b_ss, b_rs,
    ) = refs[10:36]
    rest = refs[36:]
    pc = Place()
    sums = [Total(pc, rows, rest[8 * i : 8 * i + 8]) for i, rows in enumerate([FEAT] + [CHUNK] * PARTS)]
    all_self, all_neigh = sums[0], sums[1:]

    barrier = pltpu.get_barrier_semaphore()

    def hello(to):
        pl.semaphore_signal(barrier, inc=1, device_id=to, device_id_type=MESH)

    def hello_z(d, _):
        hello(pc.along_z(d)[1])
        return _

    def hello_plane(d, _):
        hello(pc.chip(d)[1])
        return _

    lax.fori_loop(1, 8, hello_z, 0)
    lax.fori_loop(1, 16, hello_plane, 0)
    hello(pc.at(k=1 - pc.k))

    def group(s):
        return jnp.bitwise_xor(pc.zl, s)

    def adj_copy(s):
        rows = pl.ds(pl.multiple_of(group(s) * 1024, 1024), 1024)
        return pltpu.make_async_copy(adj_ref.at[rows], adj.at[rows], local_sem.at[s])

    w_copies = [pltpu.make_async_copy(ws_hbm, ws, local_sem.at[4]), pltpu.make_async_copy(wn_hbm, wn, local_sem.at[5])]
    for s in range(4):
        adj_copy(s).start()
    for copy in w_copies:
        copy.start()

    turned = og_ref[...].astype(F32).T
    grad_t[...] = turned.astype(BF16)
    scaled_t = (turned / deg_ref[...].astype(F32)).astype(BF16)
    for ch in range(PARTS):
        gath[ch, pc.zl, pc.k, pc.y] = scaled_t[ch * CHUNK : (ch + 1) * CHUNK]
    feats[pc.row] = nf_ref[...]
    lane_tile = lax.div(lax.broadcasted_iota(jnp.int32, (8, 1024), 1), 128)
    pick = (lane_tile == lax.broadcasted_iota(jnp.int32, (8, 1024), 0)).astype(F32).astype(BF16)
    wide_mask[...] = jnp.dot(mask_ref[...].astype(F32).astype(BF16), pick, preferred_element_type=F32)

    pl.semaphore_wait(barrier, 23)

    for ch in range(PARTS):
        mine = gath.at[ch, pc.zl, pc.k, pc.y]
        for s in range(1, 4):
            rdma(mine, mine, z_ss, z_rs.at[ch, s], pc.at(z=pc.zh * 4 + group(s))).start()
        for d in (1, 3, 2):
            rdma(mine, mine, y_ss, y_rs.at[ch, 0], pc.at(y=lax.rem(pc.y + d, 4))).start()
    mine = feats.at[pc.row]
    far_row = (1 - pc.zh) * 4 + pc.x
    rdma(mine, mine, f_ss.at[0], f_rs.at[0], pc.at(z=lax.rem(pc.z + 4, 8))).start()

    all_self.start(jnp.dot(grad_t[...], nf_ref[...], preferred_element_type=F32))

    def apply_mask(s):
        adj_copy(s).wait()

        def tile(t, _):
            row = group(s) * 8 + t
            rows = pl.ds(pl.multiple_of(row * 128, 128), 128)
            adj[rows, :] = adj[rows, :] * wide_mask[pl.ds(row, 1), :].astype(BF16)
            return _

        lax.fori_loop(0, 8, tile, 0)

    def forward_z(ch):
        for s in range(1, 4):
            block = gath.at[ch, group(s), pc.k, pc.y]
            pc.wait_recv(block, z_rs.at[ch, s])
            for d in (1, 3, 2):
                rdma(block, block, y_ss, y_rs.at[ch, s], pc.at(y=lax.rem(pc.y + d, 4))).start()

    def multiply(ch, s):
        g = group(s)
        pc.wait_recv(gath.at[ch, g, pc.k, pl.ds(0, 3)], y_rs.at[ch, s])
        mine = gath.at[ch, g, pc.k]
        rdma(mine, mine, k_ss, k_rs.at[ch, s], pc.at(k=1 - pc.k)).start()
        pc.wait_recv(gath.at[ch, g, 1 - pc.k], k_rs.at[ch, s])
        for y in range(4):
            for k in range(2):
                lhs[:, (2 * y + k) * 128 : (2 * y + k + 1) * 128] = gath[ch, g, k, y]

        def columns(n, _):
            lanes = pl.ds(pl.multiple_of(n * 256, 256), 256)
            rows = pl.ds(pl.multiple_of(g * 1024, 1024), 1024)
            term = jnp.dot(lhs[...], adj[rows, lanes], preferred_element_type=F32)
            acc[:, lanes] = term if s == 0 else acc[:, lanes] + term
            return _

        lax.fori_loop(0, 4, columns, 0)

    def send_rows(ch):
        for r in range(8):
            part[ch, r % 4, r // 4] = acc[:, r * 128 : (r + 1) * 128].astype(BF16)
        for d in (1, 3, 2):
            x = lax.rem(pc.x + d, 4)
            rdma(part.at[ch, x], rx.at[ch, d - 1], b_ss.at[ch, 0], b_rs.at[ch, 0], pc.at(x=x)).start()

    def neigh(ch):
        all_rows = jnp.concatenate([part[ch, r % 4, r // 4] for r in range(8)], axis=1)
        all_neigh[ch].start(jnp.dot(all_rows, feats[...].reshape(8 * NODE, FEAT), preferred_element_type=F32))

    def rows_over_x(ch):
        pc.wait_recv(rx.at[ch], b_rs.at[ch, 0])

        def total(zh):
            terms = [part[ch, pc.x, zh]] + [rx[ch, d, zh] for d in range(3)]
            return sum(t.astype(F32) for t in terms)

        zout[ch] = total(1 - pc.zh).astype(BF16)
        rdma(zout.at[ch], zin.at[ch], b_ss.at[ch, 1], b_rs.at[ch, 1], pc.at(z=lax.rem(pc.z + 4, 8))).start()
        own[...] = total(pc.zh)

    def rows_over_z(ch):
        pc.wait_recv(zin.at[ch], b_rs.at[ch, 1])
        pulled = (own[...] + zin[ch].astype(F32)).astype(BF16)
        ig_t[...] += jnp.dot(wn[:, ch * CHUNK : (ch + 1) * CHUNK], pulled, preferred_element_type=F32)

    apply_mask(0)
    forward_z(0)
    all_self.plane()
    apply_mask(1)
    multiply(0, 0)
    far = feats.at[far_row]
    pc.wait_recv(far, f_rs.at[0])
    for d in (1, 3, 2):
        to = pc.at(x=lax.rem(pc.x + d, 4))
        for block in (feats.at[pc.row], far):
            rdma(block, block, f_ss.at[1], f_rs.at[1], to).start()
    forward_z(1)
    all_self.column()
    apply_mask(2)
    apply_mask(3)
    multiply(0, 1)
    all_self.spread(factor)
    multiply(0, 2)
    all_self.cross()
    for copy in w_copies:
        copy.wait()
    ig_t[...] = jnp.dot(ws[...], grad_t[...], preferred_element_type=F32)
    multiply(0, 3)
    send_rows(0)
    pc.wait_recv(feats.at[pl.ds(0, 6)], f_rs.at[1])
    neigh(0)
    all_self.finish(gs_ref, 0)
    multiply(1, 0)
    all_neigh[0].plane()
    rows_over_x(0)
    multiply(1, 1)
    all_neigh[0].column()
    rows_over_z(0)
    multiply(1, 2)
    all_neigh[0].spread(factor)
    multiply(1, 3)
    send_rows(1)
    neigh(1)
    all_neigh[0].cross()
    all_neigh[1].plane()
    rows_over_x(1)
    all_neigh[1].column()
    all_neigh[0].finish(gn_ref, 0)
    rows_over_z(1)
    ig_ref[...] = ig_t[...].T.astype(BF16)
    all_neigh[1].spread(factor)
    all_neigh[1].cross()

    for _ in range(PARTS):
        pc.wait_send(gath.at[0, 0, 0, pl.ds(0, 3)], z_ss)
    for _ in range(PARTS):
        pc.wait_send(gath.at[0, pl.ds(0, 1), 0, pl.ds(0, 3)], y_ss)
        pc.wait_send(gath.at[0, pl.ds(0, 3), 0, pl.ds(0, 3)], y_ss)
        pc.wait_send(gath.at[0, :, 0], k_ss)
    pc.wait_send(feats.at[0], f_ss.at[0])
    pc.wait_send(feats.at[pl.ds(0, 6)], f_ss.at[1])
    for ch in range(PARTS):
        pc.wait_send(rx.at[ch], b_ss.at[ch, 0])
        pc.wait_send(zin.at[ch], b_ss.at[ch, 1])
    for one in sums:
        one.drain()
    all_neigh[1].finish(gn_ref, CHUNK)


def local(node_features, out_grad, adjacency, tile_mask, degrees, w_self, w_neigh):
    node_count = NODE * lax.axis_size("row") * lax.axis_size("col")
    factor = 1.0 / math.sqrt(node_count)
    vmem = pl.BlockSpec(memory_space=pltpu.VMEM)
    hbm = pl.BlockSpec(memory_space=pl.ANY)
    dma = pltpu.SemaphoreType.DMA
    scratch = [
        pltpu.VMEM((4096, 1024), BF16),
        pltpu.VMEM((32, 1024), F32),
        pltpu.VMEM((PARTS, 4, 2, 4, CHUNK, NODE), BF16),
        pltpu.VMEM((CHUNK, 1024), BF16),
        pltpu.VMEM((CHUNK, 1024), F32),
        pltpu.VMEM((PARTS, 4, 2, CHUNK, NODE), BF16),
        pltpu.VMEM((PARTS, 3, 2, CHUNK, NODE), BF16),
        pltpu.VMEM((PARTS, CHUNK, NODE), BF16),
        pltpu.VMEM((PARTS, CHUNK, NODE), BF16),
        pltpu.VMEM((CHUNK, NODE), F32),
        pltpu.VMEM((8, NODE, FEAT), BF16),
        pltpu.VMEM((FEAT, FEAT), BF16),
        pltpu.VMEM((FEAT, FEAT), BF16),
        pltpu.VMEM((FEAT, NODE), BF16),
        pltpu.VMEM((FEAT, NODE), F32),
        dma((6,)),
        dma,
        dma((PARTS, 4)),
        dma,
        dma((PARTS, 4)),
        dma,
        dma((PARTS, 4)),
        dma((2,)),
        dma((2,)),
        dma((PARTS, 2)),
        dma((PARTS, 2)),
    ]
    for rows in [FEAT] + [CHUNK] * PARTS:
        scratch += Total.scratch(rows)
    in_grad, self_t, neigh_t = pl.pallas_call(
        lambda *refs: kernel(factor, *refs),
        out_shape=(
            jax.ShapeDtypeStruct((NODE, FEAT), BF16),
            jax.ShapeDtypeStruct((FEAT, FEAT), BF16),
            jax.ShapeDtypeStruct((FEAT, FEAT), BF16),
        ),
        in_specs=[vmem, vmem, vmem, vmem, hbm, hbm, hbm],
        out_specs=(vmem, vmem, vmem),
        scratch_shapes=scratch,
        compiler_params=pltpu.CompilerParams(
            collective_id=0, has_side_effects=True, vmem_limit_bytes=56 * 1024 * 1024
        ),
    )(node_features, out_grad, tile_mask, degrees.reshape(1, NODE), adjacency, w_self, w_neigh)
    return in_grad, self_t.T.astype(F32), neigh_t.T.astype(F32)


def solution(mesh):
    in_specs = (
        P(("row", "col"), None),
        P(("row", "col"), None),
        P("row", "col"),
        P("row", "col"),
        P(("row", "col")),
        P(),
        P(),
    )
    out_specs = (P(("row", "col"), None), P(), P())
    return jax.shard_map(local, mesh=mesh, in_specs=in_specs, out_specs=out_specs, check_vma=False)
```

time: 457 us -> 103 us (0.23)
  waiting for transfers between devices: 418 us -> 0 us
  Pallas kernels: 0 us -> 94.9 us
  matrix products: 14.2 us -> 0 us
  between operations: 13.8 us -> 0.65 us
  other arithmetic: 6.15 us -> 1.48 us
    psum x1 -> x0, waiting for transfers between devices: 260 us -> none  [local(): self_sum, neigh_sum = lax.psum((self_part, neigh_part), ('row', 'col'))]
    pallas_call x0 -> x1, Pallas kernels: none -> 94.9 us  [local(): pl.pallas_call(lambda *refs: kernel(factor, *refs), out_shape=(jax.ShapeD...]
    reduce_scatter x1 -> x0, waiting for transfers between devices: 91.1 us -> none  [local(): lax.psum_scatter(spread_total, 'row', scatter_dimension=0, tiled=True)]
    all_gather x1 -> x0, waiting for transfers between devices: 67.1 us -> none  [local(): lax.all_gather(scaled, 'col', axis=0, tiled=True)]
    dot_general x5 -> x0, matrix products: 14.2 us -> none  [the longest x1 8.19 us: local(): lax.dot_general(edge_values, lax.all_gather(scaled, 'col', axis=0, tiled=...]
  transfers between devices with their start and end apart: 3 -> 0, of which waited for: 3 -> 0; matrix products, arithmetic and copies ran while one was open for 1% -> 0% of each run, Pallas kernels for 0% -> 0%
where the time goes in v1:
time: 103 us
  Pallas kernels  94.9 us (92%)
  local copies, waits for them, and re-layouts  5.55 us (5%)
  other arithmetic  1.48 us (1%)
    pallas_call x1, Pallas kernels, local(): pl.pallas_call(lambda *refs: kernel(factor, *refs), out_shape=(jax.ShapeD...  94.9 us
    unnamed x4, local copies, waits for them, and re-layouts  5.55 us

profile of v1, /device:TPU:1, one launch (start us, length us, event | category | flops | bytes accessed | tf_op | source)
XLA Modules:
  0.0 102.6 jit_solution(10656728897794913132)
XLA Ops:
  0.6 1.4 %copy.10.refs_2_ = s32[32,8]{1,0:T(8,128)} copy(s32[32,8]{0,1:T(8,128)} %param.10) | data formatting | bytes 2048 | tf_op args[3]
  2.0 94.9 %shard_map.94 = (bf16[128,512]{1,0:T(8,128)(2,1)}, bf16[512,512]{1,0:T(8,128)(2,1)}, bf16[512,512]{1,0:T(8,128)(2,1)}) custom-call(bf16[128,512]{1,0:T(8,128)(2,1)} %refs_0_.1, bf16[128,512]{1,0:T(8,128)(2,1)} %refs_1_.1, s32[32,8]{1,0:T(8,128)} %copy.10.refs_2_, s32[1,128]{1,0:T(1,128)} %bitcast.5, bf16[4096,1024]{1,0:T(8,128)(2,1)} %refs_4_.1, ...), custom_call_target="tpu_custom_call" | custom-call | tf_op jit(solution)/shard_map/pallas_call | solution.py:378
  96.9 1.5 %convert_bitcast_fusion = (f32[512,512]{0,1:T(8,128)S(1)}, f32[512,512]{0,1:T(8,128)S(1)}) fusion(bf16[512,512]{1,0:T(8,128)(2,1)} %get-tuple-element.8, bf16[512,512]{1,0:T(8,128)(2,1)} %get-tuple-element.7), kind=kLoop, calls=%fused_computation | loop fusion | flops 524288 | bytes 3145728 | tf_op jit(solution)/shard_map/convert_element_type | solution.py:392
  98.4 1.3 %copy.12 = f32[512,512]{1,0:T(8,128)} copy(f32[512,512]{0,1:T(8,128)S(1)} %get-tuple-element.12) | data formatting | bytes 2097152
  99.7 1.3 %copy.11 = f32[512,512]{1,0:T(8,128)} copy(f32[512,512]{0,1:T(8,128)S(1)} %get-tuple-element.13) | data formatting | bytes 2097152
  101.0 1.6 %copy.14 = bf16[128,512]{1,0:T(8,128)(2,1)} copy(bf16[128,512]{1,0:T(8,128)(2,1)} %get-tuple-element.17) | data formatting | bytes 262144

commit v2 on v1

v2 whole, which is shorter than its diff:
```python
import math

import jax
import jax.numpy as jnp
from jax import lax
from jax.experimental import pallas as pl
from jax.experimental.pallas import tpu as pltpu
from jax.sharding import PartitionSpec as P

MESH = pl.DeviceIdType.MESH
F32, BF16 = jnp.float32, jnp.bfloat16
FEAT = 512
NODE = 128
SIZES = (256, 256)
STARTS = (0, 256)
PARTS = 2
HALF = NODE // 2
SUMS = ((512, "x", "y"), (SIZES[0], "xy", None), (SIZES[1], "xy", None))


def scoped(name):
    def wrap(fn):
        def call(*args):
            with jax.named_scope(name):
                return fn(*args)

        return call

    return wrap


def rdma(src, dst, send_sem, recv_sem, to):
    return pltpu.make_async_remote_copy(
        src_ref=src, dst_ref=dst, send_sem=send_sem, recv_sem=recv_sem, device_id=to, device_id_type=MESH
    )


class Place:
    def __init__(self):
        row, col = lax.axis_index("row"), lax.axis_index("col")
        self.row, self.col = row, col
        self.x, self.zh = lax.rem(row, 4), lax.div(row, 4)
        self.zl, self.y, self.k = lax.div(col, 8), lax.rem(lax.div(col, 2), 4), lax.rem(col, 2)
        self.z = self.zh * 4 + self.zl
        self.q = self.x * 4 + self.y

    def at(self, x=None, y=None, z=None, k=None):
        x = self.x if x is None else x
        y = self.y if y is None else y
        z = self.z if z is None else z
        k = self.k if k is None else k
        return (lax.div(z, 4) * 4 + x, lax.rem(z, 4) * 8 + y * 2 + k)

    def chip(self, d):
        q = lax.rem(self.q + d, 16)
        return lax.div(q, 4), lax.rem(q, 4)

    def along(self, axis, d):
        size = 8 if axis == "z" else 4
        c = lax.rem(getattr(self, axis) + d, size)
        return c, self.at(**{axis: c})

    def wait_recv(self, ref, sem):
        rdma(ref, ref, sem, sem, self.at()).wait_recv()

    def wait_send(self, ref, sem):
        rdma(ref, ref, sem, sem, self.at()).wait_send()


class Total:
    def __init__(self, place, rows, first, second, factor, refs):
        self.place, self.rows, self.first, self.second, self.factor = place, rows, first, second, factor
        self.part, self.kin, self.out, self.in_a, self.mid, self.in_b, self.zbuf, self.whole, self.ss, self.rs = refs
        if second is None:
            self.a, self.b = place.x, place.y
        else:
            self.a, self.b = getattr(place, first), getattr(place, second)

    @staticmethod
    def scratch(rows):
        piece = (rows // 8, 128)
        return [
            pltpu.VMEM((2, rows // 2, FEAT), BF16),
            pltpu.VMEM((rows // 2, FEAT), BF16),
            pltpu.VMEM((4, 4) + piece, BF16),
            pltpu.VMEM((16,) + piece, BF16),
            pltpu.VMEM((4,) + piece, BF16),
            pltpu.VMEM((4,) + piece, BF16),
            pltpu.VMEM((8,) + piece, BF16),
            pltpu.VMEM((2, 4, 4) + piece, BF16),
            pltpu.SemaphoreType.DMA((7,)),
            pltpu.SemaphoreType.DMA((7,)),
        ]

    def spot(self, i, j):
        tall = self.rows // 8
        return slice(i * tall, (i + 1) * tall), slice(j * 128, (j + 1) * 128)

    def copy(self, n, src, dst, to):
        rdma(src, dst, self.ss.at[n], self.rs.at[n], to).start()

    @scoped("sum_start")
    def start(self):
        other = 1 - self.place.k
        self.copy(0, self.part.at[other], self.kin, self.place.at(k=other))

    @scoped("sum_first")
    def scatter(self):
        pc = self.place
        pc.wait_recv(self.kin, self.rs.at[0])
        both = (self.part[pc.k].astype(F32) + self.kin[...].astype(F32)).astype(BF16)
        for i in range(4):
            for j in range(4):
                self.out[i, j] = both[self.spot(i, j)]
        if self.second is None:

            def send(d, _):
                x, y = pc.chip(d)
                self.copy(1, self.out.at[x, y], self.in_a.at[pc.q], pc.at(x=x, y=y))
                return _

            lax.fori_loop(1, 16, send, 0)
            self.in_a[pc.q] = self.out[self.a, self.b]
        else:
            for d in (1, 3, 2):
                c, to = pc.along(self.first, d)
                self.copy(1, self.out.at[c], self.in_a.at[pl.ds(4 * self.a, 4)], to)
            self.in_a[pl.ds(4 * self.a, 4)] = self.out[self.a]

    @scoped("sum_second")
    def scatter_second(self):
        pc = self.place
        pc.wait_recv(self.in_a.at[pl.ds(0, 12)], self.rs.at[1])
        self.mid[...] = sum(self.in_a[4 * i : 4 * i + 4].astype(F32) for i in range(4)).astype(BF16)
        for d in (1, 3, 2):
            c, to = pc.along(self.second, d)
            self.copy(2, self.mid.at[c], self.in_b.at[self.b], to)
        self.in_b[self.b] = self.mid[self.b]

    @scoped("sum_column")
    def column(self):
        pc = self.place
        if self.second is None:
            self.wait_15(pc.wait_recv, self.rs.at[1])
            total = jnp.sum(self.in_a[...].astype(F32), axis=0)
        else:
            pc.wait_recv(self.in_b.at[pl.ds(0, 3)], self.rs.at[2])
            total = jnp.sum(self.in_b[...].astype(F32), axis=0)
        self.zbuf[pc.z] = total.astype(BF16)

        def send(d, _):
            self.copy(3, self.zbuf.at[pc.z], self.zbuf.at[pc.z], pc.along("z", d)[1])
            return _

        lax.fori_loop(1, 8, send, 0)

    def wait_15(self, wait, sem):
        wait(self.in_a.at[pl.ds(0, 15)], sem)

    @scoped("sum_spread")
    def spread(self):
        pc = self.place
        pc.wait_recv(self.zbuf.at[pl.ds(0, 7)], self.rs.at[3])
        self.whole[pc.k, self.a, self.b] = (jnp.sum(self.zbuf[...].astype(F32), axis=0) * self.factor).astype(BF16)
        mine = self.whole.at[pc.k, self.a, self.b]
        if self.second is None:

            def send(d, _):
                x, y = pc.chip(d)
                self.copy(4, mine, mine, pc.at(x=x, y=y))
                return _

            lax.fori_loop(1, 16, send, 0)
        else:
            for d in (1, 3, 2):
                self.copy(4, mine, mine, pc.along(self.second, d)[1])

    @scoped("sum_spread_first")
    def spread_first(self):
        pc = self.place
        pc.wait_recv(self.in_b.at[pl.ds(0, 3)], self.rs.at[4])
        mine = self.whole.at[pc.k, self.a]
        for d in (1, 3, 2):
            self.copy(5, mine, mine, pc.along(self.first, d)[1])

    @scoped("sum_cross")
    def cross(self):
        pc = self.place
        if self.second is None:
            self.wait_15(pc.wait_recv, self.rs.at[4])
        else:
            pc.wait_recv(self.in_a.at[pl.ds(0, 12)], self.rs.at[5])
        mine = self.whole.at[pc.k]
        self.copy(6, mine, mine, pc.at(k=1 - pc.k))

    @scoped("sum_finish")
    def finish(self, out_ref, base):
        pc, half = self.place, self.rows // 2
        pc.wait_recv(self.whole.at[0], self.rs.at[6])
        for h in range(2):
            for i in range(4):
                for j in range(4):
                    rows, lanes = self.spot(i, j)
                    at = base + h * half
                    out_ref[at + rows.start : at + rows.stop, lanes] = self.whole[h, i, j]

    @scoped("sum_drain")
    def drain(self):
        pc = self.place
        pc.wait_send(self.kin, self.ss.at[0])
        pc.wait_send(self.zbuf.at[pl.ds(0, 7)], self.ss.at[3])
        pc.wait_send(self.whole.at[0], self.ss.at[6])
        if self.second is None:
            self.wait_15(pc.wait_send, self.ss.at[1])
            self.wait_15(pc.wait_send, self.ss.at[4])
        else:
            pc.wait_send(self.in_a.at[pl.ds(0, 12)], self.ss.at[1])
            pc.wait_send(self.in_b.at[pl.ds(0, 3)], self.ss.at[2])
            pc.wait_send(self.in_b.at[pl.ds(0, 3)], self.ss.at[4])
            pc.wait_send(self.in_a.at[pl.ds(0, 12)], self.ss.at[5])


def kernel(factor, *refs):
    nf_ref, og_ref, mask_ref, deg_ref, adj_ref, ws_hbm, wn_hbm = refs[:7]
    ig_ref, gs_ref, gn_ref = refs[7:10]
    (
        adj, wide_mask, feats, ws, wn, grad_t, ig_t,
        local_sem, z_ss, z_rs, y_ss, near_rs, far_rs, k_ss, k_rs, f_ss, f_rs, b_ss, b_rs,
    ) = refs[10:29]
    gath, acc, part, rx, zout, zin, own = [refs[29 + i : 43 + i : 7] for i in range(7)]
    rest = refs[43:]
    pc = Place()
    all_self, early, late = [Total(pc, *spec, factor, rest[10 * i : 10 * i + 10]) for i, spec in enumerate(SUMS)]

    barrier = pltpu.get_barrier_semaphore()

    def hello(to):
        pl.semaphore_signal(barrier, inc=1, device_id=to, device_id_type=MESH)

    def hello_z(d, _):
        hello(pc.along("z", d)[1])
        return _

    def hello_plane(d, _):
        x, y = pc.chip(d)
        hello(pc.at(x=x, y=y))
        return _

    lax.fori_loop(1, 8, hello_z, 0)
    lax.fori_loop(1, 16, hello_plane, 0)
    hello(pc.at(k=1 - pc.k))

    def group(s):
        return jnp.bitwise_xor(pc.zl, s)

    def adj_copy(s):
        rows = pl.ds(pl.multiple_of(group(s) * 1024, 1024), 1024)
        return pltpu.make_async_copy(adj_ref.at[rows], adj.at[rows], local_sem.at[s])

    w_copies = [pltpu.make_async_copy(ws_hbm, ws, local_sem.at[4]), pltpu.make_async_copy(wn_hbm, wn, local_sem.at[5])]
    for s in range(4):
        adj_copy(s).start()
    for copy in w_copies:
        copy.start()

    turned = og_ref[...].astype(F32).T
    grad_t[...] = turned.astype(BF16)
    scaled_t = (turned / deg_ref[...].astype(F32)).astype(BF16)
    for ch in range(PARTS):
        gath[ch][pc.zl, pc.k, pc.y] = scaled_t[STARTS[ch] : STARTS[ch] + SIZES[ch]]
    feats[pc.row] = nf_ref[...]
    lane_tile = lax.div(lax.broadcasted_iota(jnp.int32, (8, 1024), 1), 128)
    pick = (lane_tile == lax.broadcasted_iota(jnp.int32, (8, 1024), 0)).astype(F32).astype(BF16)
    wide_mask[...] = jnp.dot(mask_ref[...].astype(F32).T.astype(BF16), pick, preferred_element_type=F32)

    def own_sum():
        value = jnp.dot(grad_t[...], nf_ref[...], preferred_element_type=F32).astype(BF16)
        all_self.part[0] = value[: FEAT // 2]
        all_self.part[1] = value[FEAT // 2 :]

    @scoped("apply_mask")
    def apply_mask(s):
        adj_copy(s).wait()

        def tile(t, _):
            row = group(s) * 8 + t
            rows = pl.ds(pl.multiple_of(row * 128, 128), 128)
            adj[rows, :] = adj[rows, :] * wide_mask[pl.ds(row, 1), :].astype(BF16)
            return _

        lax.fori_loop(0, 8, tile, 0)

    with jax.named_scope("greeting"):
        pl.semaphore_wait(barrier, 23)


    up, up_to = pc.along("y", 1)
    down, down_to = pc.along("y", 3)
    far_y = lax.rem(pc.y + 2, 4)

    def near(ch, s):
        block = gath[ch].at[group(s), pc.k, pc.y]
        rdma(block, block, y_ss, near_rs.at[ch, s], up_to).start()
        rdma(block, block, y_ss, near_rs.at[ch, s], down_to).start()

    @scoped("stage_near")
    def stage_near(ch, s):
        if s > 0:
            pc.wait_recv(gath[ch].at[group(s), pc.k, pc.y], z_rs.at[ch, s])
            near(ch, s)

    @scoped("stage_far")
    def stage_far(ch, s):
        pc.wait_recv(gath[ch].at[group(s), pc.k, pl.ds(0, 2)], near_rs.at[ch, s])
        low = gath[ch].at[group(s), pc.k, down, pl.ds(0, SIZES[ch] // 2)]
        high = gath[ch].at[group(s), pc.k, up, pl.ds(SIZES[ch] // 2, SIZES[ch] // 2)]
        rdma(low, low, y_ss, far_rs.at[ch, s], up_to).start()
        rdma(high, high, y_ss, far_rs.at[ch, s], down_to).start()

    @scoped("stage_core")
    def stage_core(ch, s):
        pc.wait_recv(gath[ch].at[group(s), pc.k, far_y], far_rs.at[ch, s])
        mine = gath[ch].at[group(s), pc.k]
        rdma(mine, mine, k_ss, k_rs.at[ch, s], pc.at(k=1 - pc.k)).start()

    @scoped("multiply")
    def multiply(ch, s):
        g = group(s)
        pc.wait_recv(gath[ch].at[g, 1 - pc.k], k_rs.at[ch, s])
        with jax.named_scope("dot"):
            rows = pl.ds(pl.multiple_of(g * 1024, 1024), 1024)
            left = jnp.concatenate([gath[ch][g, k, y] for y in range(4) for k in range(2)], axis=1)

            def columns(n, _):
                lanes = pl.ds(pl.multiple_of(n * 256, 256), 256)
                term = jnp.dot(left, adj[rows, lanes], preferred_element_type=F32)
                acc[ch][:, lanes] = term if s == 0 else acc[ch][:, lanes] + term
                return _

            lax.fori_loop(0, 4, columns, 0)

    items = [(ch, 0) for ch in range(PARTS)] + [(ch, s) for ch in range(PARTS) for s in range(1, 4)]

    @scoped("z_sends")
    def z_sends(ch):
        mine = gath[ch].at[pc.zl, pc.k, pc.y]
        for s in range(1, 4):
            rdma(mine, mine, z_ss, z_rs.at[ch, s], pc.at(z=pc.zh * 4 + group(s))).start()

    far_row = (1 - pc.zh) * 4 + pc.x
    right, right_to = pc.along("x", 1)
    left_x, left_to = pc.along("x", 3)

    @scoped("feats")
    def feats_near(n, row):
        block = feats.at[row]
        rdma(block, block, f_ss, f_rs.at[n], right_to).start()
        rdma(block, block, f_ss, f_rs.at[n], left_to).start()

    @scoped("feats")
    def feats_far(n, zh):
        pc.wait_recv(feats.at[pl.ds(0, 2)], f_rs.at[n])
        low = feats.at[zh * 4 + left_x, pl.ds(0, HALF)]
        high = feats.at[zh * 4 + right, pl.ds(HALF, HALF)]
        rdma(low, low, f_ss, f_rs.at[n + 1], right_to).start()
        rdma(high, high, f_ss, f_rs.at[n + 1], left_to).start()

    @scoped("send_rows")
    def send_rows(ch):
        for r in range(8):
            part[ch][r % 4, r // 4] = acc[ch][:, r * 128 : (r + 1) * 128].astype(BF16)

    @scoped("rows_x_start")
    def rows_x_start(ch):
        for d in (1, 3, 2):
            x, to = pc.along("x", d)
            rdma(part[ch].at[x], rx[ch].at[d - 1], b_ss.at[ch, 0], b_rs.at[ch, 0], to).start()

    @scoped("neigh")
    def neigh(ch):
        left = jnp.concatenate([part[ch][r % 4, r // 4] for r in range(8)], axis=1)
        value = jnp.dot(left, feats[...].reshape(8 * NODE, FEAT), preferred_element_type=F32)
        total = (early, late)[ch]
        total.part[0] = value[: SIZES[ch] // 2].astype(BF16)
        total.part[1] = value[SIZES[ch] // 2 :].astype(BF16)
        total.start()

    @scoped("rows_over_x")
    def rows_over_x(ch):
        pc.wait_recv(rx[ch], b_rs.at[ch, 0])

        def total(zh):
            terms = [part[ch][pc.x, zh]] + [rx[ch][d, zh] for d in range(3)]
            return sum(t.astype(F32) for t in terms)

        zout[ch][...] = total(1 - pc.zh).astype(BF16)
        rdma(zout[ch], zin[ch], b_ss.at[ch, 1], b_rs.at[ch, 1], pc.along("z", 4)[1]).start()
        own[ch][...] = total(pc.zh)

    @scoped("rows_over_z")
    def rows_over_z(ch):
        pc.wait_recv(zin[ch], b_rs.at[ch, 1])
        pulled = (own[ch][...] + zin[ch][...].astype(F32)).astype(BF16)
        ig_t[...] += jnp.dot(wn[:, STARTS[ch] : STARTS[ch] + SIZES[ch]], pulled, preferred_element_type=F32)

    @scoped("own_term")
    def own_term():
        for copy in w_copies:
            copy.wait()
        ig_t[...] = jnp.dot(ws[...], grad_t[...], preferred_element_type=F32)

    def to_far_z():
        mine = feats.at[pc.row]
        rdma(mine, mine, f_ss, f_rs.at[0], pc.along("z", 4)[1]).start()

    def from_far_z():
        pc.wait_recv(feats.at[far_row], f_rs.at[0])
        feats_near(3, far_row)

    def feats_wait():
        pc.wait_recv(feats.at[0], f_rs.at[2])
        pc.wait_recv(feats.at[0], f_rs.at[4])

    def close(ch):
        send_rows(ch)
        neigh(ch)

    def far(i):
        stage_far(*items[i])

    def forward(i):
        stage_near(*items[i])

    def core(i):
        stage_core(*items[i])

    def dot(i):
        multiply(*items[i])

    near(0, 0)
    z_sends(0)
    near(1, 0)
    feats_near(1, pc.row)
    own_sum()
    all_self.start()
    apply_mask(0)
    far(0)
    far(1)
    forward(2)
    core(0)
    forward(3)
    core(1)
    forward(4)
    to_far_z()
    z_sends(1)
    dot(0)
    far(2)
    all_self.scatter()
    dot(1)
    far(3)
    apply_mask(1)
    feats_far(1, pc.zh)
    core(2)
    far(4)
    apply_mask(2)
    apply_mask(3)
    dot(2)
    core(3)
    forward(5)
    all_self.scatter_second()
    core(4)
    dot(3)
    from_far_z()
    forward(6)
    far(5)
    own_term()
    dot(4)
    forward(7)
    send_rows(0)
    rows_x_start(0)
    core(5)
    all_self.column()
    far(6)
    feats_far(3, 1 - pc.zh)
    dot(5)
    far(7)
    core(6)
    feats_wait()
    neigh(0)
    core(7)
    dot(6)
    early.scatter()
    all_self.spread()
    rows_over_x(0)
    dot(7)
    send_rows(1)
    neigh(1)
    all_self.spread_first()
    late.scatter()
    rows_x_start(1)
    early.column()
    rows_over_z(0)
    all_self.cross()
    late.column()
    early.spread()
    all_self.finish(gs_ref, 0)
    late.spread()
    rows_over_x(1)
    early.cross()
    late.cross()
    early.finish(gn_ref, 0)
    rows_over_z(1)
    ig_ref[...] = ig_t[...].T.astype(BF16)
    late.finish(gn_ref, STARTS[1])

    with jax.named_scope("drain"):
        for blocks in gath:
            pc.wait_send(blocks.at[pl.ds(0, 3), 0, 0], z_ss)
            pc.wait_send(blocks.at[pl.ds(0, 3), 0], y_ss)
            pc.wait_send(blocks.at[:, 0], k_ss)
        pc.wait_send(feats.at[pl.ds(0, 7)], f_ss)
        for ch in range(PARTS):
            pc.wait_send(rx[ch], b_ss.at[ch, 0])
            pc.wait_send(zin[ch], b_ss.at[ch, 1])
        for total in (all_self, early, late):
            total.drain()


def finish_kernel(ig_ref, gs_ref, gn_ref, ig_out, gs_out, gn_out):
    ig_out[...] = ig_ref[...]
    gs_out[...] = gs_ref[...].astype(F32).T
    gn_out[...] = gn_ref[...].astype(F32).T


def local(node_features, out_grad, adjacency, tile_mask, degrees, w_self, w_neigh):
    node_count = NODE * lax.axis_size("row") * lax.axis_size("col")
    factor = 1.0 / math.sqrt(node_count)
    vmem = pl.BlockSpec(memory_space=pltpu.VMEM)
    hbm = pl.BlockSpec(memory_space=pl.ANY)
    dma = pltpu.SemaphoreType.DMA
    scratch = [
        pltpu.VMEM((4096, 1024), BF16),
        pltpu.VMEM((32, 1024), F32),
        pltpu.VMEM((8, NODE, FEAT), BF16),
        pltpu.VMEM((FEAT, FEAT), BF16),
        pltpu.VMEM((FEAT, FEAT), BF16),
        pltpu.VMEM((FEAT, NODE), BF16),
        pltpu.VMEM((FEAT, NODE), F32),
        dma((6,)),
        dma,
        dma((PARTS, 4)),
        dma,
        dma((PARTS, 4)),
        dma((PARTS, 4)),
        dma,
        dma((PARTS, 4)),
        dma,
        dma((5,)),
        dma((PARTS, 2)),
        dma((PARTS, 2)),
    ]
    for size in SIZES:
        scratch += [
            pltpu.VMEM((4, 2, 4, size, NODE), BF16),
            pltpu.VMEM((size, 1024), F32),
            pltpu.VMEM((4, 2, size, NODE), BF16),
            pltpu.VMEM((3, 2, size, NODE), BF16),
            pltpu.VMEM((size, NODE), BF16),
            pltpu.VMEM((size, NODE), BF16),
            pltpu.VMEM((size, NODE), F32),
        ]
    for rows, _, _ in SUMS:
        scratch += Total.scratch(rows)
    shapes = [pltpu.VMEM((n, FEAT), BF16) for n in (NODE, FEAT, FEAT)]
    results = pl.pallas_call(
        lambda *refs: kernel(factor, *refs),
        out_shape=shapes,
        in_specs=[vmem, vmem, vmem, vmem, hbm, hbm, hbm],
        out_specs=(vmem, vmem, vmem),
        scratch_shapes=scratch,
        compiler_params=pltpu.CompilerParams(
            collective_id=0, has_side_effects=True, vmem_limit_bytes=56 * 1024 * 1024
        ),
    )(node_features, out_grad, tile_mask.T, degrees.reshape(1, NODE), adjacency, w_self, w_neigh)
    return pl.pallas_call(
        finish_kernel,
        out_shape=[jax.ShapeDtypeStruct((n, FEAT), t) for n, t in ((NODE, BF16), (FEAT, F32), (FEAT, F32))],
        in_specs=[vmem] * 3,
        out_specs=[vmem] * 3,
        compiler_params=pltpu.CompilerParams(vmem_limit_bytes=16 * 1024 * 1024),
    )(*results)


def solution(mesh):
    in_specs = (
        P(("row", "col"), None),
        P(("row", "col"), None),
        P("row", "col"),
        P("row", "col"),
        P(("row", "col")),
        P(),
        P(),
    )
    out_specs = (P(("row", "col"), None), P(), P())
    return jax.shard_map(local, mesh=mesh, in_specs=in_specs, out_specs=out_specs, check_vma=False)
```

time: 103 us -> 72.5 us (0.70)
  Pallas kernels: 94.9 us -> 71.8 us
  local copies, waits for them, and re-layouts: 5.55 us -> 0 us
  other arithmetic: 1.48 us -> 0 us
    pallas_call x1 -> x2, Pallas kernels: 94.9 us -> 71.8 us  [the longest x1 70.1 us: local(): pl.pallas_call(lambda *refs: kernel(factor, *refs), out_shape=shapes, in_...]
    unnamed x4 -> x0, local copies, waits for them, and re-layouts: 5.55 us -> none
    convert_element_type x1 -> x0, other arithmetic: 1.48 us -> none  [local(): return (in_grad, self_t.T.astype(F32), neigh_t.T.astype(F32))]
where the time goes in v2:
time: 72.5 us; the launch traced here: 72.4 us
  Pallas kernels  71.8 us (99%)
    pallas_call x1, Pallas kernels, local(): pl.pallas_call(lambda *refs: kernel(factor, *refs), out_shape=shapes, in_...  70.1 us
    pallas_call x1, Pallas kernels, local(): pl.pallas_call(finish_kernel, out_shape=[jax.ShapeDtypeStruct((n, FEAT),...  1.65 us

profile of v2, /device:TPU:1, one launch (start us, length us, event | category | flops | bytes accessed | tf_op | source)
XLA Modules:
  0.0 72.4 jit_solution(18412779827349842248)
XLA Ops:
  0.6 70.1 %shard_map.94 = (bf16[128,512]{1,0:T(8,128)(2,1)S(1)}, bf16[512,512]{1,0:T(8,128)(2,1)S(1)}, bf16[512,512]{1,0:T(8,128)(2,1)S(1)}) custom-call(bf16[128,512]{1,0:T(8,128)(2,1)} %refs_0_.1, bf16[128,512]{1,0:T(8,128)(2,1)} %refs_1_.1, s32[8,32]{1,0:T(8,128)} %bitcast.2, s32[1,128]{1,0:T(1,128)} %bitcast.3, bf16[4096,1024]{1,0:T(8,128)(2,1)} %refs_4_.1, ...), custom_call_target="tpu_custom_call" | custom-call | tf_op jit(solution)/shard_map/pallas_call | solution.py:575
  70.8 1.6 %shard_map.95 = (bf16[128,512]{1,0:T(8,128)(2,1)}, f32[512,512]{1,0:T(8,128)}, f32[512,512]{1,0:T(8,128)}) custom-call(bf16[128,512]{1,0:T(8,128)(2,1)S(1)} %get-tuple-element.6.ig_ref, bf16[512,512]{1,0:T(8,128)(2,1)S(1)} %get-tuple-element.7.gs_ref, bf16[512,512]{1,0:T(8,128)(2,1)S(1)} %get-tuple-element.8.gn_ref), custom_call_target="tpu_custom_call" | custom-call | tf_op jit(solution)/shard_map/pallas_call | solution.py:585

commit v3 on v2

--- a/solution.py
+++ b/solution.py
@@ -15,7 +15,7 @@
 STARTS = (0, 256)
 PARTS = 2
 HALF = NODE // 2
-SUMS = ((512, "x", "y"), (SIZES[0], "xy", None), (SIZES[1], "xy", None))
+SUMS = ((512, "x", "y", True), (SIZES[0], "xy", None, False), (SIZES[1], "xy", None, False))
 
 
 def scoped(name):
@@ -68,8 +68,8 @@
 
 
 class Total:
-    def __init__(self, place, rows, first, second, factor, refs):
-        self.place, self.rows, self.first, self.second, self.factor = place, rows, first, second, factor
+    def __init__(self, place, rows, first, second, turn, factor, refs):
+        self.place, self.rows, self.first, self.second, self.turn, self.factor = place, rows, first, second, turn, factor
         self.part, self.kin, self.out, self.in_a, self.mid, self.in_b, self.zbuf, self.whole, self.ss, self.rs = refs
         if second is None:
             self.a, self.b = place.x, place.y
@@ -173,15 +173,15 @@
             lax.fori_loop(1, 16, send, 0)
         else:
             for d in (1, 3, 2):
-                self.copy(4, mine, mine, pc.along(self.second, d)[1])
+                self.copy(4, mine, mine, pc.along(self.first if self.turn else self.second, d)[1])
 
     @scoped("sum_spread_first")
     def spread_first(self):
         pc = self.place
         pc.wait_recv(self.in_b.at[pl.ds(0, 3)], self.rs.at[4])
-        mine = self.whole.at[pc.k, self.a]
+        mine = self.whole.at[pc.k, :, self.b] if self.turn else self.whole.at[pc.k, self.a]
         for d in (1, 3, 2):
-            self.copy(5, mine, mine, pc.along(self.first, d)[1])
+            self.copy(5, mine, mine, pc.along(self.second if self.turn else self.first, d)[1])
 
     @scoped("sum_cross")
     def cross(self):
@@ -221,14 +221,14 @@
 
 
 def kernel(factor, *refs):
-    nf_ref, og_ref, mask_ref, deg_ref, adj_ref, ws_hbm, wn_hbm = refs[:7]
+    nf_hbm, og_hbm, mask_hbm, deg_hbm, adj_ref, ws_hbm, wn_hbm = refs[:7]
     ig_ref, gs_ref, gn_ref = refs[7:10]
     (
-        adj, wide_mask, feats, ws, wn, grad_t, ig_t,
+        adj, wide_mask, feats, ws, wn, grad_t, ig_t, og_ref, mask_ref, deg_ref,
         local_sem, z_ss, z_rs, y_ss, near_rs, far_rs, k_ss, k_rs, f_ss, f_rs, b_ss, b_rs,
-    ) = refs[10:29]
-    gath, acc, part, rx, zout, zin, own = [refs[29 + i : 43 + i : 7] for i in range(7)]
-    rest = refs[43:]
+    ) = refs[10:32]
+    gath, acc, part, rx, zout, zin, own = [refs[32 + i : 46 + i : 7] for i in range(7)]
+    rest = refs[46:]
     pc = Place()
     all_self, early, late = [Total(pc, *spec, factor, rest[10 * i : 10 * i + 10]) for i, spec in enumerate(SUMS)]
 
@@ -258,23 +258,31 @@
         return pltpu.make_async_copy(adj_ref.at[rows], adj.at[rows], local_sem.at[s])
 
     w_copies = [pltpu.make_async_copy(ws_hbm, ws, local_sem.at[4]), pltpu.make_async_copy(wn_hbm, wn, local_sem.at[5])]
+    small = [(og_hbm, og_ref), (deg_hbm, deg_ref), (nf_hbm, feats.at[pc.row]), (mask_hbm, mask_ref)]
+    in_copies = [pltpu.make_async_copy(src, dst, local_sem.at[6 + i]) for i, (src, dst) in enumerate(small)]
+    for copy in in_copies:
+        copy.start()
     for s in range(4):
         adj_copy(s).start()
     for copy in w_copies:
         copy.start()
+    in_copies[0].wait()
+    in_copies[1].wait()
 
     turned = og_ref[...].astype(F32).T
     grad_t[...] = turned.astype(BF16)
     scaled_t = (turned / deg_ref[...].astype(F32)).astype(BF16)
     for ch in range(PARTS):
         gath[ch][pc.zl, pc.k, pc.y] = scaled_t[STARTS[ch] : STARTS[ch] + SIZES[ch]]
-    feats[pc.row] = nf_ref[...]
-    lane_tile = lax.div(lax.broadcasted_iota(jnp.int32, (8, 1024), 1), 128)
-    pick = (lane_tile == lax.broadcasted_iota(jnp.int32, (8, 1024), 0)).astype(F32).astype(BF16)
-    wide_mask[...] = jnp.dot(mask_ref[...].astype(F32).T.astype(BF16), pick, preferred_element_type=F32)
+
+    def spread_mask():
+        in_copies[3].wait()
+        lane_tile = lax.div(lax.broadcasted_iota(jnp.int32, (8, 1024), 1), 128)
+        pick = (lane_tile == lax.broadcasted_iota(jnp.int32, (8, 1024), 0)).astype(F32).astype(BF16)
+        wide_mask[...] = jnp.dot(mask_ref[...].astype(F32).T.astype(BF16), pick, preferred_element_type=F32)
 
     def own_sum():
-        value = jnp.dot(grad_t[...], nf_ref[...], preferred_element_type=F32).astype(BF16)
+        value = jnp.dot(grad_t[...], feats[pc.row], preferred_element_type=F32).astype(BF16)
         all_self.part[0] = value[: FEAT // 2]
         all_self.part[1] = value[FEAT // 2 :]
 
@@ -300,8 +308,8 @@
 
     def near(ch, s):
         block = gath[ch].at[group(s), pc.k, pc.y]
-        rdma(block, block, y_ss, near_rs.at[ch, s], up_to).start()
-        rdma(block, block, y_ss, near_rs.at[ch, s], down_to).start()
+        for d in (1, 3, 2):
+            rdma(block, block, y_ss, near_rs.at[ch, s], pc.along("y", d)[1]).start()
 
     @scoped("stage_near")
     def stage_near(ch, s):
@@ -309,17 +317,12 @@
             pc.wait_recv(gath[ch].at[group(s), pc.k, pc.y], z_rs.at[ch, s])
             near(ch, s)
 
-    @scoped("stage_far")
     def stage_far(ch, s):
-        pc.wait_recv(gath[ch].at[group(s), pc.k, pl.ds(0, 2)], near_rs.at[ch, s])
-        low = gath[ch].at[group(s), pc.k, down, pl.ds(0, SIZES[ch] // 2)]
-        high = gath[ch].at[group(s), pc.k, up, pl.ds(SIZES[ch] // 2, SIZES[ch] // 2)]
-        rdma(low, low, y_ss, far_rs.at[ch, s], up_to).start()
-        rdma(high, high, y_ss, far_rs.at[ch, s], down_to).start()
+        pass
 
     @scoped("stage_core")
     def stage_core(ch, s):
-        pc.wait_recv(gath[ch].at[group(s), pc.k, far_y], far_rs.at[ch, s])
+        pc.wait_recv(gath[ch].at[group(s), pc.k, pl.ds(0, 3)], near_rs.at[ch, s])
         mine = gath[ch].at[group(s), pc.k]
         rdma(mine, mine, k_ss, k_rs.at[ch, s], pc.at(k=1 - pc.k)).start()
 
@@ -439,13 +442,15 @@
 
     near(0, 0)
     z_sends(0)
+    in_copies[2].wait()
+    own_sum()
+    all_self.start()
+    spread_mask()
+    apply_mask(0)
     near(1, 0)
     feats_near(1, pc.row)
-    own_sum()
-    all_self.start()
-    apply_mask(0)
-    far(0)
-    far(1)
+    apply_mask(1)
+    apply_mask(2)
     forward(2)
     core(0)
     forward(3)
@@ -454,59 +459,51 @@
     to_far_z()
     z_sends(1)
     dot(0)
-    far(2)
     all_self.scatter()
+    core(2)
     dot(1)
-    far(3)
-    apply_mask(1)
     feats_far(1, pc.zh)
-    core(2)
-    far(4)
-    apply_mask(2)
+    core(3)
     apply_mask(3)
     dot(2)
-    core(3)
+    core(4)
+    from_far_z()
     forward(5)
     all_self.scatter_second()
-    core(4)
     dot(3)
-    from_far_z()
     forward(6)
-    far(5)
     own_term()
     dot(4)
     forward(7)
     send_rows(0)
+    feats_far(3, 1 - pc.zh)
     rows_x_start(0)
     core(5)
     all_self.column()
-    far(6)
-    feats_far(3, 1 - pc.zh)
+    core(6)
     dot(5)
-    far(7)
-    core(6)
     feats_wait()
     neigh(0)
     core(7)
     dot(6)
     early.scatter()
     all_self.spread()
-    rows_over_x(0)
     dot(7)
     send_rows(1)
     neigh(1)
+    rows_over_x(0)
+    late.scatter()
+    early.column()
+    rows_x_start(1)
     all_self.spread_first()
-    late.scatter()
-    rows_x_start(1)
-    early.column()
     rows_over_z(0)
-    all_self.cross()
     late.column()
     early.spread()
+    all_self.cross()
+    rows_over_x(1)
+    late.spread()
+    early.cross()
     all_self.finish(gs_ref, 0)
-    late.spread()
-    rows_over_x(1)
-    early.cross()
     late.cross()
     early.finish(gn_ref, 0)
     rows_over_z(1)
@@ -546,7 +543,10 @@
         pltpu.VMEM((FEAT, FEAT), BF16),
         pltpu.VMEM((FEAT, NODE), BF16),
         pltpu.VMEM((FEAT, NODE), F32),
-        dma((6,)),
+        pltpu.VMEM((NODE, FEAT), BF16),
+        pltpu.VMEM((8, 32), jnp.int32),
+        pltpu.VMEM((1, NODE), jnp.int32),
+        dma((10,)),
         dma,
         dma((PARTS, 4)),
         dma,
@@ -569,13 +569,13 @@
             pltpu.VMEM((size, NODE), BF16),
             pltpu.VMEM((size, NODE), F32),
         ]
-    for rows, _, _ in SUMS:
+    for rows, _, _, _ in SUMS:
         scratch += Total.scratch(rows)
     shapes = [pltpu.VMEM((n, FEAT), BF16) for n in (NODE, FEAT, FEAT)]
     results = pl.pallas_call(
         lambda *refs: kernel(factor, *refs),
         out_shape=shapes,
-        in_specs=[vmem, vmem, vmem, vmem, hbm, hbm, hbm],
+        in_specs=[hbm] * 7,
         out_specs=(vmem, vmem, vmem),
         scratch_shapes=scratch,
         compiler_params=pltpu.CompilerParams(

time: 72.5 us -> 64.6 us (0.89)
  Pallas kernels: 71.8 us -> 63.9 us
    pallas_call x1, Pallas kernels: 70.1 us -> 62.3 us  [local(): pl.pallas_call(lambda *refs: kernel(factor, *refs), out_shape=shapes, in_...]
where the time goes in v3:
time: 64.6 us
  Pallas kernels  63.9 us (99%)
    pallas_call x1, Pallas kernels, local(): pl.pallas_call(lambda *refs: kernel(factor, *refs), out_shape=shapes, in_...  62.3 us
    pallas_call x1, Pallas kernels, local(): pl.pallas_call(finish_kernel, out_shape=[jax.ShapeDtypeStruct((n, FEAT),...  1.65 us

profile of v3, /device:TPU:1, one launch (start us, length us, event | category | flops | bytes accessed | tf_op | source)
XLA Modules:
  0.0 64.6 jit_solution(10115115469746444315)
XLA Ops:
  0.6 62.3 %shard_map.94 = (bf16[128,512]{1,0:T(8,128)(2,1)S(1)}, bf16[512,512]{1,0:T(8,128)(2,1)S(1)}, bf16[512,512]{1,0:T(8,128)(2,1)S(1)}) custom-call(bf16[128,512]{1,0:T(8,128)(2,1)} %refs_0_.1, bf16[128,512]{1,0:T(8,128)(2,1)} %refs_1_.1, s32[8,32]{1,0:T(8,128)} %bitcast.2, s32[1,128]{1,0:T(1,128)} %bitcast.3, bf16[4096,1024]{1,0:T(8,128)(2,1)} %refs_4_.1, ...), custom_call_target="tpu_custom_call" | custom-call | tf_op jit(solution)/shard_map/pallas_call | solution.py:575
  62.9 1.6 %shard_map.95 = (bf16[128,512]{1,0:T(8,128)(2,1)}, f32[512,512]{1,0:T(8,128)}, f32[512,512]{1,0:T(8,128)}) custom-call(bf16[128,512]{1,0:T(8,128)(2,1)S(1)} %get-tuple-element.6.ig_ref, bf16[512,512]{1,0:T(8,128)(2,1)S(1)} %get-tuple-element.7.gs_ref, bf16[512,512]{1,0:T(8,128)(2,1)S(1)} %get-tuple-element.8.gn_ref), custom_call_target="tpu_custom_call" | custom-call | tf_op jit(solution)/shard_map/pallas_call | solution.py:585

commit v4 on v3

--- a/solution.py
+++ b/solution.py
@@ -11,11 +11,11 @@
 F32, BF16 = jnp.float32, jnp.bfloat16
 FEAT = 512
 NODE = 128
-SIZES = (256, 256)
-STARTS = (0, 256)
-PARTS = 2
+SIZES = (256, 128, 128)
+STARTS = (0, 256, 384)
+PARTS = 3
 HALF = NODE // 2
-SUMS = ((512, "x", "y", True), (SIZES[0], "xy", None, False), (SIZES[1], "xy", None, False))
+SUMS = ((512, "x", "y", True), (384, "xy", None, False), (128, "xy", None, False))
 
 
 def scoped(name):
@@ -80,7 +80,7 @@
     def scratch(rows):
         piece = (rows // 8, 128)
         return [
-            pltpu.VMEM((2, rows // 2, FEAT), BF16),
+            pltpu.VMEM((rows, FEAT), BF16),
             pltpu.VMEM((rows // 2, FEAT), BF16),
             pltpu.VMEM((4, 4) + piece, BF16),
             pltpu.VMEM((16,) + piece, BF16),
@@ -102,13 +102,17 @@
     @scoped("sum_start")
     def start(self):
         other = 1 - self.place.k
-        self.copy(0, self.part.at[other], self.kin, self.place.at(k=other))
+        self.copy(0, self.part.at[self.half(other)], self.kin, self.place.at(k=other))
+
+    def half(self, k):
+        rows = self.rows // 2
+        return pl.ds(pl.multiple_of(k * rows, rows), rows)
 
     @scoped("sum_first")
     def scatter(self):
         pc = self.place
         pc.wait_recv(self.kin, self.rs.at[0])
-        both = (self.part[pc.k].astype(F32) + self.kin[...].astype(F32)).astype(BF16)
+        both = (self.part[self.half(pc.k), :].astype(F32) + self.kin[...].astype(F32)).astype(BF16)
         for i in range(4):
             for j in range(4):
                 self.out[i, j] = both[self.spot(i, j)]
@@ -227,8 +231,8 @@
         adj, wide_mask, feats, ws, wn, grad_t, ig_t, og_ref, mask_ref, deg_ref,
         local_sem, z_ss, z_rs, y_ss, near_rs, far_rs, k_ss, k_rs, f_ss, f_rs, b_ss, b_rs,
     ) = refs[10:32]
-    gath, acc, part, rx, zout, zin, own = [refs[32 + i : 46 + i : 7] for i in range(7)]
-    rest = refs[46:]
+    gath, acc, part, rx, zout, zin, own = [refs[32 + i : 53 + i : 7] for i in range(7)]
+    rest = refs[53:]
     pc = Place()
     all_self, early, late = [Total(pc, *spec, factor, rest[10 * i : 10 * i + 10]) for i, spec in enumerate(SUMS)]
 
@@ -282,9 +286,7 @@
         wide_mask[...] = jnp.dot(mask_ref[...].astype(F32).T.astype(BF16), pick, preferred_element_type=F32)
 
     def own_sum():
-        value = jnp.dot(grad_t[...], feats[pc.row], preferred_element_type=F32).astype(BF16)
-        all_self.part[0] = value[: FEAT // 2]
-        all_self.part[1] = value[FEAT // 2 :]
+        all_self.part[...] = jnp.dot(grad_t[...], feats[pc.row], preferred_element_type=F32).astype(BF16)
 
     @scoped("apply_mask")
     def apply_mask(s):
@@ -334,13 +336,8 @@
             rows = pl.ds(pl.multiple_of(g * 1024, 1024), 1024)
             left = jnp.concatenate([gath[ch][g, k, y] for y in range(4) for k in range(2)], axis=1)
 
-            def columns(n, _):
-                lanes = pl.ds(pl.multiple_of(n * 256, 256), 256)
-                term = jnp.dot(left, adj[rows, lanes], preferred_element_type=F32)
-                acc[ch][:, lanes] = term if s == 0 else acc[ch][:, lanes] + term
-                return _
-
-            lax.fori_loop(0, 4, columns, 0)
+            term = jnp.dot(left, adj[rows, :], preferred_element_type=F32)
+            acc[ch][...] = term if s == 0 else acc[ch][...] + term
 
     items = [(ch, 0) for ch in range(PARTS)] + [(ch, s) for ch in range(PARTS) for s in range(1, 4)]
 
@@ -383,10 +380,12 @@
     def neigh(ch):
         left = jnp.concatenate([part[ch][r % 4, r // 4] for r in range(8)], axis=1)
         value = jnp.dot(left, feats[...].reshape(8 * NODE, FEAT), preferred_element_type=F32)
-        total = (early, late)[ch]
-        total.part[0] = value[: SIZES[ch] // 2].astype(BF16)
-        total.part[1] = value[SIZES[ch] // 2 :].astype(BF16)
-        total.start()
+        if ch < 2:
+            early.part[STARTS[ch] : STARTS[ch] + SIZES[ch]] = value.astype(BF16)
+        else:
+            late.part[...] = value.astype(BF16)
+        if ch > 0:
+            (early if ch == 1 else late).start()
 
     @scoped("rows_over_x")
     def rows_over_x(ch):
@@ -448,67 +447,85 @@
     spread_mask()
     apply_mask(0)
     near(1, 0)
+    near(2, 0)
     feats_near(1, pc.row)
     apply_mask(1)
     apply_mask(2)
-    forward(2)
+    forward(3)
     core(0)
-    forward(3)
+    forward(4)
     core(1)
-    forward(4)
+    core(2)
+    forward(5)
     to_far_z()
     z_sends(1)
+    z_sends(2)
     dot(0)
     all_self.scatter()
-    core(2)
+    core(3)
     dot(1)
     feats_far(1, pc.zh)
-    core(3)
+    core(4)
+    dot(2)
     apply_mask(3)
-    dot(2)
-    core(4)
+    dot(3)
+    core(5)
     from_far_z()
-    forward(5)
+    forward(6)
     all_self.scatter_second()
-    dot(3)
-    forward(6)
-    own_term()
     dot(4)
     forward(7)
+    forward(8)
+    own_term()
+    dot(5)
+    forward(9)
+    forward(10)
+    core(6)
     send_rows(0)
     feats_far(3, 1 - pc.zh)
     rows_x_start(0)
-    core(5)
+    forward(11)
+    core(7)
     all_self.column()
-    core(6)
-    dot(5)
+    core(8)
+    dot(6)
+    core(9)
+    dot(7)
     feats_wait()
     neigh(0)
-    core(7)
-    dot(6)
-    early.scatter()
-    all_self.spread()
-    dot(7)
+    core(10)
+    dot(8)
     send_rows(1)
     neigh(1)
+    core(11)
+    all_self.spread()
+    dot(9)
+    early.scatter()
+    dot(10)
+    dot(11)
+    send_rows(2)
+    neigh(2)
     rows_over_x(0)
     late.scatter()
+    rows_x_start(1)
     early.column()
-    rows_x_start(1)
-    all_self.spread_first()
+    rows_x_start(2)
     rows_over_z(0)
     late.column()
+    all_self.spread_first()
     early.spread()
-    all_self.cross()
     rows_over_x(1)
     late.spread()
+    rows_over_x(2)
     early.cross()
+    all_self.cross()
+    rows_over_z(1)
+    late.cross()
     all_self.finish(gs_ref, 0)
-    late.cross()
     early.finish(gn_ref, 0)
-    rows_over_z(1)
+    rows_over_z(2)
     ig_ref[...] = ig_t[...].T.astype(BF16)
-    late.finish(gn_ref, STARTS[1])
+    late.finish(gn_ref, STARTS[2])
 
     with jax.named_scope("drain"):
         for blocks in gath:

time: 64.6 us -> 64 us (level)
  no operation moved by 1% of the time
where the time goes in v4:
time: 64 us; the launch traced here: 63.9 us
  Pallas kernels  63.3 us (99%)
  between operations  0.64 us (1%)
    pallas_call x1, Pallas kernels, local(): pl.pallas_call(lambda *refs: kernel(factor, *refs), out_shape=shapes, in_...  61.7 us
    pallas_call x1, Pallas kernels, local(): pl.pallas_call(finish_kernel, out_shape=[jax.ShapeDtypeStruct((n, FEAT),...  1.65 us

profile of v4, /device:TPU:1, one launch (start us, length us, event | category | flops | bytes accessed | tf_op | source)
XLA Modules:
  0.0 63.9 jit_solution(16394378054939847398)
XLA Ops:
  0.6 61.7 %shard_map.94 = (bf16[128,512]{1,0:T(8,128)(2,1)S(1)}, bf16[512,512]{1,0:T(8,128)(2,1)S(1)}, bf16[512,512]{1,0:T(8,128)(2,1)S(1)}) custom-call(bf16[128,512]{1,0:T(8,128)(2,1)} %refs_0_.1, bf16[128,512]{1,0:T(8,128)(2,1)} %refs_1_.1, s32[8,32]{1,0:T(8,128)} %bitcast.2, s32[1,128]{1,0:T(1,128)} %bitcast.3, bf16[4096,1024]{1,0:T(8,128)(2,1)} %refs_4_.1, ...), custom_call_target="tpu_custom_call" | custom-call | tf_op jit(solution)/shard_map/pallas_call | solution.py:592
  62.3 1.6 %shard_map.95 = (bf16[128,512]{1,0:T(8,128)(2,1)}, f32[512,512]{1,0:T(8,128)}, f32[512,512]{1,0:T(8,128)}) custom-call(bf16[128,512]{1,0:T(8,128)(2,1)S(1)} %get-tuple-element.6.ig_ref, bf16[512,512]{1,0:T(8,128)(2,1)S(1)} %get-tuple-element.7.gs_ref, bf16[512,512]{1,0:T(8,128)(2,1)S(1)} %get-tuple-element.8.gn_ref), custom_call_target="tpu_custom_call" | custom-call | tf_op jit(solution)/shard_map/pallas_call | solution.py:602

commit v5 on v4

--- a/solution.py
+++ b/solution.py
@@ -119,7 +119,7 @@
         if self.second is None:
 
             def send(d, _):
-                x, y = pc.chip(d)
+                x, y = pc.chip(lax.rem(d + 8, 15) + 1)
                 self.copy(1, self.out.at[x, y], self.in_a.at[pc.q], pc.at(x=x, y=y))
                 return _
 
@@ -153,7 +153,7 @@
         self.zbuf[pc.z] = total.astype(BF16)
 
         def send(d, _):
-            self.copy(3, self.zbuf.at[pc.z], self.zbuf.at[pc.z], pc.along("z", d)[1])
+            self.copy(3, self.zbuf.at[pc.z], self.zbuf.at[pc.z], pc.along("z", lax.rem(d + 2, 7) + 1)[1])
             return _
 
         lax.fori_loop(1, 8, send, 0)
@@ -170,7 +170,7 @@
         if self.second is None:
 
             def send(d, _):
-                x, y = pc.chip(d)
+                x, y = pc.chip(lax.rem(d + 8, 15) + 1)
                 self.copy(4, mine, mine, pc.at(x=x, y=y))
                 return _
 

time: 64 us -> 62.8 us (0.981)
  Pallas kernels: 63.3 us -> 62 us
    pallas_call x1, Pallas kernels: 61.7 us -> 60.4 us  [local(): pl.pallas_call(lambda *refs: kernel(factor, *refs), out_shape=shapes, in_...]
where the time goes in v5:
time: 62.8 us; the launch traced here: 62.7 us
  Pallas kernels  62 us (99%)
  between operations  0.64 us (1%)
    pallas_call x1, Pallas kernels, local(): pl.pallas_call(lambda *refs: kernel(factor, *refs), out_shape=shapes, in_...  60.4 us
    pallas_call x1, Pallas kernels, local(): pl.pallas_call(finish_kernel, out_shape=[jax.ShapeDtypeStruct((n, FEAT),...  1.65 us

profile of v5, /device:TPU:1, one launch (start us, length us, event | category | flops | bytes accessed | tf_op | source)
XLA Modules:
  0.0 62.7 jit_solution(17506595758619122338)
XLA Ops:
  0.6 60.4 %shard_map.94 = (bf16[128,512]{1,0:T(8,128)(2,1)S(1)}, bf16[512,512]{1,0:T(8,128)(2,1)S(1)}, bf16[512,512]{1,0:T(8,128)(2,1)S(1)}) custom-call(bf16[128,512]{1,0:T(8,128)(2,1)} %refs_0_.1, bf16[128,512]{1,0:T(8,128)(2,1)} %refs_1_.1, s32[8,32]{1,0:T(8,128)} %bitcast.2, s32[1,128]{1,0:T(1,128)} %bitcast.3, bf16[4096,1024]{1,0:T(8,128)(2,1)} %refs_4_.1, ...), custom_call_target="tpu_custom_call" | custom-call | tf_op jit(solution)/shard_map/pallas_call | solution.py:592
  61.0 1.6 %shard_map.95 = (bf16[128,512]{1,0:T(8,128)(2,1)}, f32[512,512]{1,0:T(8,128)}, f32[512,512]{1,0:T(8,128)}) custom-call(bf16[128,512]{1,0:T(8,128)(2,1)S(1)} %get-tuple-element.6.ig_ref, bf16[512,512]{1,0:T(8,128)(2,1)S(1)} %get-tuple-element.7.gs_ref, bf16[512,512]{1,0:T(8,128)(2,1)S(1)} %get-tuple-element.8.gn_ref), custom_call_target="tpu_custom_call" | custom-call | tf_op jit(solution)/shard_map/pallas_call | solution.py:602
